TPU v7x, 256 devices: a whole 4x4x8 slice. The times are simulated.
256 devices in a mesh: seq: 64 (over y_lo, x, z), dp: 4 (over y_hi, core).
Axes of the slice: x: 4, y: 4 (y_hi: 2, y_lo: 2; y = y_hi * 2 + y_lo), z: 8, core: 2. Of those that a mesh axis runs over, the one named last changes fastest.
Arguments:
- signal: float32 [4, 65536, 384], P('dp', 'seq'), may hold values from -6 to 6
- gate_values: float32 [4, 65536, 384], P('dp', 'seq'), may hold values from -6 to 6
- cotangent: float32 [4, 65536, 384], P('dp', 'seq'), may hold values from -6 to 6
- kernel: float32 [128, 512, 384], P(None, 'seq'), may hold values from -6 to 6
- first_factor: float32 [128, 128], replicated, may hold values from -0.5 to 0.5
- second_factor: float32 [512, 512], replicated, may hold values from -0.25 to 0.25
Outputs:
- grad_signal: float32 [4, 65536, 384], P('dp', 'seq')
- grad_gates: float32 [4, 65536, 384], P('dp', 'seq')
- grad_kernel: float32 [128, 512, 384], P('dp', 'seq')
- grad_first: float32 [128, 128], replicated
- grad_second: float32 [512, 512], replicated
All inputs are finite; a program needn't handle non-finite values.
Results may differ from a plain program's by a relative error of at most 0.000071.
Values sent between devices are 32-bit elements; how exact they have to be, the bound alone decides.
No kernel may reach another device: no remote copies, remote signals or barrier semaphores. Data moves between devices by JAX's collectives and lax.ppermute only.
A program may use at most 128 MiB of HBM per device.

v0:
```python
import math

import jax
import jax.numpy as jnp
from jax import lax
from jax.sharding import PartitionSpec as P


def along_second(data, factor):
    return jnp.einsum("bijc,kj->bikc", data, factor, precision=lax.Precision.HIGHEST)


def along_second_t(data, factor):
    return jnp.einsum("bikc,kj->bijc", data, factor, precision=lax.Precision.HIGHEST)


def along_first(factor, data):
    return jnp.einsum("mi,bikc->bmkc", factor, data, precision=lax.Precision.HIGHEST)


def along_first_t(factor, data):
    return jnp.einsum("mi,bmkc->bikc", factor, data, precision=lax.Precision.HIGHEST)


def outer_first(left, right):
    return jnp.einsum("bmkc,bikc->mi", left, right, precision=lax.Precision.HIGHEST)


def outer_second(left, right):
    return jnp.einsum("bikc,bijc->kj", left, right, precision=lax.Precision.HIGHEST)


def body(signal, gate_values, cotangent, kernel, first_factor, second_factor):
    batch = signal.shape[0]
    blocks = first_factor.shape[0]
    block = second_factor.shape[0]
    channels = signal.shape[2]
    local_rows = signal.shape[1] // block
    shape_rows = (batch, local_rows, block, channels)
    source = signal.reshape(shape_rows)
    gating = gate_values.reshape(shape_rows)
    upstream = cotangent.reshape(shape_rows)
    whole = lax.all_to_all(source, "seq", split_axis=3, concat_axis=1, tiled=True)
    kernel_cols = lax.all_to_all(kernel, "seq", split_axis=2, concat_axis=1, tiled=True)
    section_one = along_second(whole, second_factor)
    spectrum = along_first(first_factor, section_one)
    weighted = kernel_cols[None] * spectrum
    back_one = along_first_t(first_factor, weighted)
    full_mixed = along_second_t(back_one, second_factor)
    mixed = lax.all_to_all(full_mixed, "seq", split_axis=1, concat_axis=3, tiled=True)
    grad_mixed = upstream * gating
    grad_gate = upstream * mixed
    grad_whole = lax.all_to_all(grad_mixed, "seq", split_axis=3, concat_axis=1, tiled=True)
    grad_back = along_second(grad_whole, second_factor)
    second_grad = outer_second(back_one, grad_whole)
    grad_weighted = along_first(first_factor, grad_back)
    first_grad = outer_first(weighted, grad_back)
    kernel_cols_grad = jnp.sum(grad_weighted * spectrum, axis=0)
    grad_spectrum = grad_weighted * kernel_cols[None]
    grad_section = along_first_t(first_factor, grad_spectrum)
    first_grad = first_grad + outer_first(grad_spectrum, section_one)
    grad_full = along_second_t(grad_section, second_factor)
    second_grad = second_grad + outer_second(grad_section, whole)
    grad_source = lax.all_to_all(grad_full, "seq", split_axis=1, concat_axis=3, tiled=True)
    kernel_term = lax.all_to_all(kernel_cols_grad, "seq", split_axis=1, concat_axis=2, tiled=True)
    grad_kernel = lax.psum_scatter(kernel_term, "dp", scatter_dimension=0, tiled=True)
    first_total, second_total = lax.psum((first_grad, second_grad), ("seq", "dp"))
    sequences = batch * lax.axis_size("dp")
    first_scale = 1.0 / math.sqrt(sequences * block * channels)
    second_scale = 1.0 / math.sqrt(sequences * blocks * channels)
    return (
        grad_source.reshape(signal.shape),
        grad_gate.reshape(signal.shape),
        grad_kernel,
        first_total * first_scale,
        second_total * second_scale,
    )


def solution(mesh):
    in_specs = (
        P("dp", "seq", None),
        P("dp", "seq", None),
        P("dp", "seq", None),
        P(None, "seq", None),
        P(),
        P(),
    )
    out_specs = (P("dp", "seq", None), P("dp", "seq", None), P("dp", "seq", None), P(), P())
    return jax.shard_map(body, mesh=mesh, in_specs=in_specs, out_specs=out_specs, check_vma=False)
```

profile of v0, /device:TPU:6, one launch (start us, length us, event | category | flops | bytes accessed | tf_op | source)
XLA Modules:
  0.0 535.5 jit_solution(2666855981043520354)
XLA Ops:
  8.0 3.8 copy.114
  11.8 13.0 %all-to-all-start.3 = ((f32[1,2,512,384]{2,1,0,3:T(2,128)}), f32[1,2,512,384]{2,1,0,3:T(2,128)S(1)}, u32[]{:S(2)}, u32[]{:S(2)}) async-start(f32[1,2,512,384]{2,1,0,3:T(2,128)} %copy.114), calls=%async_computation.3 | async-start | bytes 3145728 | tf_op jit(solution)/shard_map/all_to_all | solution.py:43
  24.8 3.2 mul.41
  28.0 3.7 copy.113
  31.7 32.9 %all-to-all-done.3 = f32[1,2,512,384]{2,1,0,3:T(2,128)S(1)} async-done(((f32[1,2,512,384]{2,1,0,3:T(2,128)}), f32[1,2,512,384]{2,1,0,3:T(2,128)S(1)}, u32[]{:S(2)}, u32[]{:S(2)}) %all-to-all-start.3) | async-done | bytes 1572896 | tf_op jit(solution)/shard_map/all_to_all | solution.py:43
  64.6 6.6 %all-to-all-start = ((f32[1,2,512,384]{2,1,0,3:T(2,128)}), f32[1,2,512,384]{2,1,0,3:T(2,128)}, u32[]{:S(2)}, u32[]{:S(2)}) async-start(f32[1,2,512,384]{2,1,0,3:T(2,128)} %copy.113), calls=%async_computation | async-start | bytes 3145728 | tf_op jit(solution)/shard_map/all_to_all | solution.py:53
  74.3 35.7 %all-to-all-done = f32[1,2,512,384]{2,1,0,3:T(2,128)} async-done(((f32[1,2,512,384]{2,1,0,3:T(2,128)}), f32[1,2,512,384]{2,1,0,3:T(2,128)}, u32[]{:S(2)}, u32[]{:S(2)}) %all-to-all-start) | async-done | bytes 1572896 | tf_op jit(solution)/shard_map/all_to_all | solution.py:53
  110.0 6.3 %all-to-all-start.1 = ((f32[128,8,384]{0,1,2:T(8,128)}), f32[128,8,384]{0,1,2:T(8,128)S(1)}, u32[]{:S(2)}, u32[]{:S(2)}) async-start(f32[128,8,384]{0,1,2:T(8,128)} %copy.87), calls=%async_computation.1 | async-start | bytes 3145728 | tf_op jit(solution)/shard_map/all_to_all | solution.py:44
  119.4 3.1 reshape.99
  125.6 3.3 reshape.93
  129.0 4.2 fusion.44
  143.9 10.8 %all-to-all-done.1 = f32[128,8,384]{0,1,2:T(8,128)S(1)} async-done(((f32[128,8,384]{0,1,2:T(8,128)}), f32[128,8,384]{0,1,2:T(8,128)S(1)}, u32[]{:S(2)}, u32[]{:S(2)}) %all-to-all-start.1) | async-done | bytes 1572896 | tf_op jit(solution)/shard_map/all_to_all | solution.py:44
  154.6 6.9 %all-to-all-start.5 = ((f32[128,512,6]{0,2,1:T(8,128)}), f32[128,512,6]{0,2,1:T(8,128)}, u32[]{:S(2)}, u32[]{:S(2)}) async-start(f32[128,512,6]{0,2,1:T(8,128)} %copy.98), calls=%async_computation.5 | async-start | bytes 4194304 | tf_op jit(solution)/shard_map/all_to_all | solution.py:65
  171.1 38.3 %all-to-all-done.5 = f32[128,512,6]{0,2,1:T(8,128)} async-done(((f32[128,512,6]{0,2,1:T(8,128)}), f32[128,512,6]{0,2,1:T(8,128)}, u32[]{:S(2)}, u32[]{:S(2)}) %all-to-all-start.5) | async-done | bytes 1572896 | tf_op jit(solution)/shard_map/all_to_all | solution.py:65
  209.4 6.8 %all-to-all-start.4 = ((f32[1,128,512,6]{2,0,3,1:T(1,128)}), f32[1,128,512,6]{2,0,3,1:T(1,128)}, u32[]{:S(2)}, u32[]{:S(2)}) async-start(f32[1,128,512,6]{2,0,3,1:T(1,128)} %copy.95), calls=%async_computation.4 | async-start | bytes 3145728 | tf_op jit(solution)/shard_map/all_to_all | solution.py:50
  216.6 4.7 fusion.25
  225.6 3.4 fusion.40
  229.0 3.7 fusion.31
  243.5 9.3 %all-to-all-done.4 = f32[1,128,512,6]{2,0,3,1:T(1,128)} async-done(((f32[1,128,512,6]{2,0,3,1:T(1,128)}), f32[1,128,512,6]{2,0,3,1:T(1,128)}, u32[]{:S(2)}, u32[]{:S(2)}) %all-to-all-start.4) | async-done | bytes 1572896 | tf_op jit(solution)/shard_map/all_to_all | solution.py:50
  252.7 6.8 %all-to-all-start.2 = ((f32[1,128,512,6]{2,0,3,1:T(1,128)}), f32[1,128,512,6]{2,0,3,1:T(1,128)S(1)}, u32[]{:S(2)}, u32[]{:S(2)}) async-start(f32[1,128,512,6]{2,0,3,1:T(1,128)} %copy.90), calls=%async_computation.2 | async-start | bytes 3145728 | tf_op jit(solution)/shard_map/all_to_all | solution.py:64
  262.6 242.0 %all-reduce.3.cloned.1.call-done = (f32[128,128]{1,0:T(8,128)}, f32[512,512]{1,0:T(8,128)}) async-done(((f32[128,128]{1,0:T(8,128)}, f32[512,512]{1,0:T(8,128)}), (f32[128,128]{1,0:T(8,128)}, f32[512,512]{1,0:T(8,128)})) %all-reduce.3.cloned.1.call-update) | async-done | bytes 1114128 | tf_op jit(solution)/shard_map/psum | solution.py:67
  508.4 3.4 copy.124
  511.8 3.4 all_to_all.85
  515.2 3.4 mul.45
  (62 shorter events, 60.9 us)
Async XLA Ops:
  8.0 120.9 %copy-start = (f32[512,512]{1,0:T(8,128)S(1)}, f32[512,512]{1,0:T(8,128)}, u32[]{:S(2)}) copy-start(f32[512,512]{1,0:T(8,128)} %param.11) | copy-start | bytes 3145732
  11.8 52.8 %all-to-all-start.3 = ((f32[1,2,512,384]{2,1,0,3:T(2,128)}), f32[1,2,512,384]{2,1,0,3:T(2,128)S(1)}, u32[]{:S(2)}, u32[]{:S(2)}) async-start(f32[1,2,512,384]{2,1,0,3:T(2,128)} %copy.114), calls=%async_computation.3 | async-start | bytes 3145728 | tf_op jit(solution)/shard_map/all_to_all | solution.py:43
  64.6 9.7 %copy-start.14 = (f32[1,2,512,384]{2,1,0,3:T(2,128)}, f32[1,2,512,384]{2,1,0,3:T(2,128)S(1)}, u32[]{:S(2)}) copy-start(f32[1,2,512,384]{2,1,0,3:T(2,128)S(1)} %all-to-all-done.3) | copy-start | bytes 4718596
  64.6 45.4 %all-to-all-start = ((f32[1,2,512,384]{2,1,0,3:T(2,128)}), f32[1,2,512,384]{2,1,0,3:T(2,128)}, u32[]{:S(2)}, u32[]{:S(2)}) async-start(f32[1,2,512,384]{2,1,0,3:T(2,128)} %copy.113), calls=%async_computation | async-start | bytes 3145728 | tf_op jit(solution)/shard_map/all_to_all | solution.py:53
  110.0 44.6 %all-to-all-start.1 = ((f32[128,8,384]{0,1,2:T(8,128)}), f32[128,8,384]{0,1,2:T(8,128)S(1)}, u32[]{:S(2)}, u32[]{:S(2)}) async-start(f32[128,8,384]{0,1,2:T(8,128)} %copy.87), calls=%async_computation.1 | async-start | bytes 3145728 | tf_op jit(solution)/shard_map/all_to_all | solution.py:44
  128.9 4.2 copy-start.15
  133.2 1.5 copy-start.6
  133.2 2.0 copy-start.8
  135.2 5.3 copy-start.3
  137.8 2.6 copy-start.9
  140.5 1.1 copy-start.1
  154.6 54.7 %all-to-all-start.5 = ((f32[128,512,6]{0,2,1:T(8,128)}), f32[128,512,6]{0,2,1:T(8,128)}, u32[]{:S(2)}, u32[]{:S(2)}) async-start(f32[128,512,6]{0,2,1:T(8,128)} %copy.98), calls=%async_computation.5 | async-start | bytes 4194304 | tf_op jit(solution)/shard_map/all_to_all | solution.py:65
  164.3 1.2 copy-start.13
  209.4 43.4 %all-to-all-start.4 = ((f32[1,128,512,6]{2,0,3,1:T(1,128)}), f32[1,128,512,6]{2,0,3,1:T(1,128)}, u32[]{:S(2)}, u32[]{:S(2)}) async-start(f32[1,128,512,6]{2,0,3,1:T(1,128)} %copy.95), calls=%async_computation.4 | async-start | bytes 3145728 | tf_op jit(solution)/shard_map/all_to_all | solution.py:50
  216.2 288.4 %all-reduce.3.cloned.1.call-start = ((), (), s32[]{:S(2)}) async-start(), calls=%async_computation.8 | async-start | bytes 2228224 | tf_op jit(solution)/shard_map/psum | solution.py:67
  216.6 4.7 copy-start.4
  216.6 4.7 copy-start.10
  221.4 2.7 copy-start.2
  224.1 1.4 copy-start.7
  225.6 3.4 copy-start.11
  225.6 3.4 copy-start.5
  232.7 295.1 %reduce-scatter.2.cloned.1.call-start = ((), (), s32[]{:S(2)}) async-start(), calls=%async_computation.7 | async-start | bytes 1966080 | tf_op jit(solution)/shard_map/reduce_scatter | solution.py:66
  236.7 1.4 copy-start.12
  252.7 268.8 %all-to-all-start.2 = ((f32[1,128,512,6]{2,0,3,1:T(1,128)}), f32[1,128,512,6]{2,0,3,1:T(1,128)S(1)}, u32[]{:S(2)}, u32[]{:S(2)}) async-start(f32[1,128,512,6]{2,0,3,1:T(1,128)} %copy.90), calls=%async_computation.2 | async-start | bytes 3145728 | tf_op jit(solution)/shard_map/all_to_all | solution.py:64
Sparse Core Ops, SparseCore 0:
  232.8 271.7 all-reduce.2
Sparse Core Ops, SparseCore 1:
  236.8 48.6 reduce-scatter.1
where the time goes:
time: 543 us; the launch traced here: 535 us
  waiting for transfers between devices  369 us (68%)
  local copies, waits for them, and re-layouts  57.9 us (11%)
  starting transfers between devices  47 us (9%)
  matrix products  35 us (6%)
  between operations  16 us (3%)
  other arithmetic  10.5 us (2%)
    psum x1, waiting for transfers between devices, body(): lax.psum((first_grad, second_grad), ('seq', 'dp'))  242 us
    all_to_all x1, waiting for transfers between devices, body(): lax.all_to_all(kernel_cols_grad, 'seq', split_axis=1, concat_axis=2, tile...  38.3 us
    all_to_all x1, waiting for transfers between devices, body(): lax.all_to_all(grad_mixed, 'seq', split_axis=3, concat_axis=1, tiled=True)  35.7 us
    all_to_all x1, waiting for transfers between devices, body(): lax.all_to_all(source, 'seq', split_axis=3, concat_axis=1, tiled=True)  32.9 us
    unnamed x36, local copies, waits for them, and re-layouts  14.9 us
    all_to_all x1, starting transfers between devices, body(): lax.all_to_all(source, 'seq', split_axis=3, concat_axis=1, tiled=True)  13 us
  transfers between devices with their start and end apart: 8, of which 6 were waited for; matrix products, arithmetic and copies ran while one was open for 17% of the time, Pallas kernels for 0%

commit v1 on v0

v1 whole, which is shorter than its diff:
```python
import math

import jax
import jax.numpy as jnp
from jax import lax
from jax.experimental import pallas as pl
from jax.experimental.pallas import tpu as pltpu
from jax.sharding import Mesh, PartitionSpec as P

F32 = jnp.float32
BF16 = jnp.bfloat16
VMEM = pl.BlockSpec(memory_space=pltpu.VMEM)
PARAMS = pltpu.CompilerParams(vmem_limit_bytes=48 * 1024 * 1024)


def halves(value):
    high = value.astype(BF16)
    return high, (value - high.astype(F32)).astype(BF16)


def product(left, right, dims):
    one = lambda a, b: lax.dot_general(a, b, (dims, ((), ())), preferred_element_type=F32)
    return one(left[0], right[0]) + (one(left[0], right[1]) + one(left[1], right[0]))


NN = ((1,), (0,))
TN = ((0,), (0,))
NT = ((1,), (1,))


def enter_kernel(x_ref, s_ref, out_ref):
    rows, block, channels = x_ref.shape
    second = halves(s_ref[...])
    for row in range(rows):
        got = product(second, halves(x_ref[row]), NN)
        out_ref[:, row] = got.reshape(out_ref.shape[0], out_ref.shape[2], channels)


def enter_gated_kernel(g_ref, c_ref, s_ref, out_ref):
    rows, block, channels = g_ref.shape
    second = halves(s_ref[...])
    for row in range(rows):
        got = product(second, halves(g_ref[row] * c_ref[row]), NN)
        out_ref[:, row] = got.reshape(out_ref.shape[0], out_ref.shape[2], channels)


def forward_kernel(a_ref, k_ref, f_ref, z_ref, v_ref):
    first = halves(f_ref[...])
    for k in range(a_ref.shape[1]):
        z = product(first, halves(a_ref[:, k]), NN)
        z_ref[:, k] = z
        v_ref[:, k] = product(first, halves(k_ref[:, k] * z), TN)


def backward_kernel(a_ref, d_ref, k_ref, z_ref, f_ref, da_ref, gk_ref, gf_ref):
    first = halves(f_ref[...])
    total = jnp.zeros(gf_ref.shape, F32)
    for k in range(a_ref.shape[1]):
        dv = halves(d_ref[:, k])
        dw = product(first, dv, NN)
        z = z_ref[:, k]
        weight = k_ref[:, k]
        gk_ref[:, k] = dw * z
        dz = halves(weight * dw)
        da_ref[:, k] = product(first, dz, TN)
        total += product(halves(weight * z), dv, NT) + product(dz, halves(a_ref[:, k]), NT)
    gf_ref[...] = total


def leave_gates_kernel(v_ref, g_ref, c_ref, s_ref, gg_ref, gs_ref):
    rows, block, channels = g_ref.shape
    second = halves(s_ref[...])
    total = jnp.zeros(gs_ref.shape, F32)
    for row in range(rows):
        v = halves(v_ref[:, row].reshape(block, channels))
        gg_ref[row] = c_ref[row] * product(second, v, TN)
        total += product(v, halves(g_ref[row] * c_ref[row]), NT)
    gs_ref[...] = total


def leave_signal_kernel(d_ref, x_ref, s_ref, gx_ref, gs_ref):
    rows, block, channels = x_ref.shape
    second = halves(s_ref[...])
    total = jnp.zeros(gs_ref.shape, F32)
    for row in range(rows):
        d = halves(d_ref[:, row].reshape(block, channels))
        gx_ref[row] = product(second, d, TN)
        total += product(d, halves(x_ref[row]), NT)
    gs_ref[...] = total


def call(kernel, outs, *args):
    return pl.pallas_call(
        kernel,
        out_shape=[jax.ShapeDtypeStruct(shape, F32) for shape in outs],
        in_specs=[VMEM] * len(args),
        out_specs=[VMEM] * len(outs),
        compiler_params=PARAMS,
    )(*args)


def exchange(data, axes):
    return lax.all_to_all(data, axes, split_axis=0, concat_axis=0, tiled=True)


def scatter_sum(data, axes):
    parts = lax.axis_size(axes)
    got = exchange(data, axes)
    return jnp.sum(got.reshape((parts, got.shape[0] // parts) + got.shape[1:]), axis=0)


def gather(data, axes):
    parts = lax.axis_size(axes)
    return exchange(jnp.broadcast_to(data[None], (parts,) + data.shape).reshape((parts * data.shape[0],) + data.shape[1:]), axes)


def total_of(data, stages):
    for axes in stages:
        data = scatter_sum(data, axes)
    for axes in reversed(stages):
        data = gather(data, axes)
    return data


def solution(mesh):
    seq = ("near", "x", "z")
    dp = ("far", "core")
    shape = dict(mesh.shape)
    near = 2
    xs = 4
    fine = Mesh(
        mesh.devices.reshape(near, xs, shape["seq"] // (near * xs), shape["dp"] // 2, 2),
        seq + dp,
    )

    def body(signal, gate_values, cotangent, kernel, first_factor, second_factor):
        blocks = first_factor.shape[0]
        block = second_factor.shape[0]
        channels = signal.shape[2]
        peers = lax.axis_size(seq)
        rows = signal.shape[1] // block
        width = block // peers
        send = (peers, rows, width, channels)
        side = (blocks, width, channels)
        place = (rows, block, channels)
        source = signal.reshape(place)
        gating = gate_values.reshape(place)
        upstream = cotangent.reshape(place)
        (section,) = call(enter_kernel, [send], source, second_factor)
        section = exchange(section, seq).reshape(side)
        (grad_back,) = call(enter_gated_kernel, [send], gating, upstream, second_factor)
        grad_back = exchange(grad_back, seq).reshape(side)
        spectrum, back = call(forward_kernel, [side, side], section, kernel, first_factor)
        back = exchange(back.reshape(send), seq)
        grad_section, grad_kernel, grad_first = call(
            backward_kernel, [side, side, (blocks, blocks)], section, grad_back, kernel, spectrum, first_factor
        )
        grad_section = exchange(grad_section.reshape(send), seq)
        grad_kernel = scatter_sum(grad_kernel, dp)
        grad_gate, second_one = call(
            leave_gates_kernel, [place, (block, block)], back, gating, upstream, second_factor
        )
        grad_source, second_two = call(
            leave_signal_kernel, [place, (block, block)], grad_section, source, second_factor
        )
        sequences = lax.axis_size(dp)
        first_scale = 1.0 / math.sqrt(sequences * block * channels)
        second_scale = 1.0 / math.sqrt(sequences * blocks * channels)
        stages = (("near", "x", "far"), ("z", "core"))
        pieces = 1
        for axes in stages:
            pieces *= lax.axis_size(axes)
        first_total = total_of(grad_first.reshape(pieces, -1), stages).reshape(grad_first.shape)
        second_total = total_of((second_one + second_two).reshape(pieces, -1), stages).reshape(block, block)
        return (
            grad_source.reshape(signal.shape),
            grad_gate.reshape(signal.shape),
            grad_kernel,
            first_total * first_scale,
            second_total * second_scale,
        )

    wide = P(dp, seq, None)
    return jax.shard_map(
        body,
        mesh=fine,
        in_specs=(wide, wide, wide, P(None, seq, None), P(), P()),
        out_specs=(wide, wide, wide, P(), P()),
        check_vma=False,
    )
```

time: 543 us -> 372 us (0.69)
  waiting for transfers between devices: 369 us -> 170 us
  blocking collectives: 0 us -> 66.3 us
  Pallas kernels: 0 us -> 43.2 us
  local copies, waits for them, and re-layouts: 57.9 us -> 21.2 us
  matrix products: 35 us -> 0 us
  between operations: 16 us -> 1.3 us
  starting transfers between devices: 47 us -> 61.5 us
  other arithmetic: 10.5 us -> 3.4 us
    psum x1 -> x0, waiting for transfers between devices: 242 us -> none  [body(): lax.psum((first_grad, second_grad), ('seq', 'dp'))]
    all_to_all x0 -> x3, blocking collectives: none -> 66.3 us  [exchange(): return lax.all_to_all(data, axes, split_axis=0, concat_axis=0, tiled=True)]
    pallas_call x0 -> x6, Pallas kernels: none -> 43.2 us  [call(): pl.pallas_call(kernel, out_shape=[jax.ShapeDtypeStruct(shape, F32) for sh...]
    all_to_all x6 -> x10, waiting for transfers between devices: 127 us -> 170 us  [exchange(): return lax.all_to_all(data, axes, split_axis=0, concat_axis=0, tiled=True)]
    dot_general x12 -> x0, matrix products: 35 us -> none  [the longest x2 8.4 us: outer_second(): jnp.einsum('bikc,bijc->kj', left, right, precision=lax.Precision.HIGHEST)]
    all_to_all x7 -> x4, local copies, waits for them, and re-layouts: 18.6 us -> 2.57 us  [exchange(): return lax.all_to_all(data, axes, split_axis=0, concat_axis=0, tiled=True)]
    all_to_all x6 -> x10, starting transfers between devices: 46.3 us -> 61.5 us  [exchange(): return lax.all_to_all(data, axes, split_axis=0, concat_axis=0, tiled=True)]
    reshape x3 -> x2, local copies, waits for them, and re-layouts: 9.69 us -> 0.64 us  [gather(): jnp.broadcast_to(data[None], (parts,) + data.shape)]
  transfers between devices with their start and end apart: 8 -> 10, of which waited for: 6 -> 9; matrix products, arithmetic and copies ran while one was open for 17% -> 1% of each run, Pallas kernels for 0% -> 5%
where the time goes in v1:
time: 372 us; the launch traced here: 367 us
  waiting for transfers between devices  170 us (46%)
  blocking collectives  66.3 us (18%)
  starting transfers between devices  61.5 us (17%)
  Pallas kernels  43.2 us (12%)
  local copies, waits for them, and re-layouts  21.2 us (6%)
    all_to_all x10, waiting for transfers between devices, exchange(): return lax.all_to_all(data, axes, split_axis=0, concat_axis=0, tiled=True)  170 us
    all_to_all x3, blocking collectives, exchange(): return lax.all_to_all(data, axes, split_axis=0, concat_axis=0, tiled=True)  66.3 us
    all_to_all x10, starting transfers between devices, exchange(): return lax.all_to_all(data, axes, split_axis=0, concat_axis=0, tiled=True)  61.5 us
    pallas_call x6, Pallas kernels, call(): pl.pallas_call(kernel, out_shape=[jax.ShapeDtypeStruct(shape, F32) for sh...  43.2 us
    unnamed x33, local copies, waits for them, and re-layouts  15 us
  transfers between devices with their start and end apart: 10, of which 9 were waited for; matrix products, arithmetic and copies ran while one was open for 1% of the time, Pallas kernels for 5%

profile of v1, /device:TPU:6, one launch (start us, length us, event | category | flops | bytes accessed | tf_op | source)
XLA Modules:
  0.0 366.8 jit_solution(3121261361308488603)
XLA Ops:
  6.2 13.1 %all-to-all-start = ((f32[64,2,8,384]{3,2,1,0:T(8,128)}), f32[64,2,8,384]{3,2,1,0:T(8,128)S(1)}, u32[]{:S(2)}, u32[]{:S(2)}) async-start(f32[64,2,8,384]{3,2,1,0:T(8,128)} %copy-done.4), calls=%async_computation | async-start | bytes 3145728 | tf_op jit(solution)/shard_map/all_to_all | solution.py:103
  25.2 34.0 %all-to-all-done = f32[64,2,8,384]{3,2,1,0:T(8,128)S(1)} async-done(((f32[64,2,8,384]{3,2,1,0:T(8,128)}), f32[64,2,8,384]{3,2,1,0:T(8,128)S(1)}, u32[]{:S(2)}, u32[]{:S(2)}) %all-to-all-start) | async-done | bytes 1572896 | tf_op jit(solution)/shard_map/all_to_all | solution.py:103
  59.1 6.8 %all-to-all-start.1 = ((f32[64,2,8,384]{3,2,1,0:T(8,128)}), f32[64,2,8,384]{3,2,1,0:T(8,128)}, u32[]{:S(2)}, u32[]{:S(2)}) async-start(f32[64,2,8,384]{3,2,1,0:T(8,128)} %copy-done.3), calls=%async_computation.1 | async-start | bytes 3145728 | tf_op jit(solution)/shard_map/all_to_all | solution.py:103
  65.9 8.3 %shard_map.103 = (f32[128,8,384]{2,1,0:T(8,128)S(1)}, f32[128,8,384]{2,1,0:T(8,128)S(1)}) custom-call(f32[128,8,384]{2,1,0:T(8,128)S(1)} %bitcast.15, f32[128,8,384]{2,1,0:T(8,128)} %k_ref.3, f32[128,128]{1,0:T(8,128)S(1)} %copy-done.13), custom_call_target="tpu_custom_call" | custom-call | tf_op jit(solution)/shard_map/pallas_call | solution.py:93
  76.5 28.0 %all-to-all-done.1 = f32[64,2,8,384]{3,2,1,0:T(8,128)} async-done(((f32[64,2,8,384]{3,2,1,0:T(8,128)}), f32[64,2,8,384]{3,2,1,0:T(8,128)}, u32[]{:S(2)}, u32[]{:S(2)}) %all-to-all-start.1) | async-done | bytes 1572896 | tf_op jit(solution)/shard_map/all_to_all | solution.py:103
  104.6 22.3 %shard_map.104 = (f32[128,8,384]{2,1,0:T(8,128)S(1)}, f32[128,8,384]{2,1,0:T(8,128)}, f32[128,128]{1,0:T(8,128)S(1)}) custom-call(f32[128,8,384]{2,1,0:T(8,128)S(1)} %bitcast.16, f32[128,8,384]{2,1,0:T(8,128)} %bitcast.4.d_ref, f32[128,8,384]{2,1,0:T(8,128)} %k_ref.3, f32[128,8,384]{2,1,0:T(8,128)} %copy-done.12, f32[128,128]{1,0:T(8,128)S(1)} %copy-done.13), custom_call_target="tpu_custom_call" | custom-call | tf_op jit(solution)/shard_map/pallas_call | solution.py:93
  128.2 12.5 %all_to_all.85 = f32[16,1,1024]{2,1,0:T(1,128)S(1)} all-to-all(f32[16,1,1024]{2,1,0:T(1,128)S(1)} %reshape.116), channel_id=1, replica_groups=mesh['near'=2,'x'=4,'z'=8,'far'=2,'core'=2] {'near','x','far'}, dimensions={0} | all-to-all | bytes 131072 | tf_op jit(solution)/shard_map/all_to_all | solution.py:103
  140.7 43.5 %all_to_all.86.d_ref = f32[64,2,8,384]{3,2,1,0:T(8,128)} all-to-all(f32[64,2,8,384]{3,2,1,0:T(8,128)} %bitcast.24), channel_id=1, replica_groups=mesh['near'=2,'x'=4,'z'=8,'far'=2,'core'=2] {'near','x','z'}, dimensions={0} | all-to-all | bytes 3145728 | tf_op jit(solution)/shard_map/all_to_all | solution.py:103
  184.2 6.3 %all-to-all-start.3 = ((f32[64,2,8,384]{3,2,1,0:T(8,128)}), f32[64,2,8,384]{3,2,1,0:T(8,128)S(1)}, u32[]{:S(2)}, u32[]{:S(2)}) async-start(f32[64,2,8,384]{3,2,1,0:T(8,128)} %bitcast.23), calls=%async_computation.3 | async-start | bytes 3145728 | tf_op jit(solution)/shard_map/all_to_all | solution.py:103
  192.4 33.9 %all-to-all-done.3.v_ref = f32[64,2,8,384]{3,2,1,0:T(8,128)S(1)} async-done(((f32[64,2,8,384]{3,2,1,0:T(8,128)}), f32[64,2,8,384]{3,2,1,0:T(8,128)S(1)}, u32[]{:S(2)}, u32[]{:S(2)}) %all-to-all-start.3) | async-done | bytes 1572896 | tf_op jit(solution)/shard_map/all_to_all | solution.py:103
  232.6 3.8 %shard_map.105 = (f32[2,512,384]{2,1,0:T(8,128)}, f32[512,512]{1,0:T(8,128)S(1)}) custom-call(f32[64,2,8,384]{3,2,1,0:T(8,128)S(1)} %copy-done.2, f32[2,512,384]{2,1,0:T(8,128)S(1)} %bitcast.18, f32[512,512]{1,0:T(8,128)S(1)} %copy-done.1), custom_call_target="tpu_custom_call" | custom-call | tf_op jit(solution)/shard_map/pallas_call | solution.py:93
  236.4 5.2 %shard_map.106 = (f32[2,512,384]{2,1,0:T(8,128)}, f32[512,512]{1,0:T(8,128)S(1)}) custom-call(f32[64,2,8,384]{3,2,1,0:T(8,128)S(1)} %all-to-all-done.3.v_ref, f32[2,512,384]{2,1,0:T(8,128)S(1)} %bitcast.20, f32[2,512,384]{2,1,0:T(8,128)} %bitcast.21, f32[512,512]{1,0:T(8,128)S(1)} %copy-done.1), custom_call_target="tpu_custom_call" | custom-call | tf_op jit(solution)/shard_map/pallas_call | solution.py:93
  243.1 6.7 %all-to-all-start.9 = ((f32[16,16,1024]{2,1,0:T(8,128)}), f32[16,16,1024]{2,1,0:T(8,128)S(1)}, u32[]{:S(2)}, u32[]{:S(2)}) async-start(f32[16,16,1024]{2,1,0:T(8,128)} %all_to_all.66), calls=%async_computation.9 | async-start | bytes 2097152 | tf_op jit(solution)/shard_map/all_to_all | solution.py:103
  249.8 18.0 %all-to-all-done.9 = f32[16,16,1024]{2,1,0:T(8,128)S(1)} async-done(((f32[16,16,1024]{2,1,0:T(8,128)}), f32[16,16,1024]{2,1,0:T(8,128)S(1)}, u32[]{:S(2)}, u32[]{:S(2)}) %all-to-all-start.9) | async-done | bytes 1048608 | tf_op jit(solution)/shard_map/all_to_all | solution.py:103
  268.4 6.8 %all-to-all-start.7 = ((f32[16,1,64]{2,1,0:T(1,128)}), f32[16,1,64]{2,1,0:T(1,128)S(1)}, u32[]{:S(2)}, u32[]{:S(2)}) async-start(f32[16,1,64]{2,1,0:T(1,128)} %reshape.114), calls=%async_computation.7 | async-start | bytes 16384 | tf_op jit(solution)/shard_map/all_to_all | solution.py:103
  276.0 6.8 %all-to-all-done.7 = f32[16,1,64]{2,1,0:T(1,128)S(1)} async-done(((f32[16,1,64]{2,1,0:T(1,128)}), f32[16,1,64]{2,1,0:T(1,128)S(1)}, u32[]{:S(2)}, u32[]{:S(2)}) %all-to-all-start.7) | async-done | bytes 4128 | tf_op jit(solution)/shard_map/all_to_all | solution.py:103
  287.1 7.0 %all-to-all-done.10 = f32[16,1,1024]{2,1,0:T(1,128)S(1)} async-done(((f32[16,1,1024]{2,1,0:T(1,128)}), f32[16,1,1024]{2,1,0:T(1,128)S(1)}, u32[]{:S(2)}, u32[]{:S(2)}) %all-to-all-start.10) | async-done | bytes 65568 | tf_op jit(solution)/shard_map/all_to_all | solution.py:103
  294.1 5.6 %all-to-all-start.8 = ((f32[16,1,1024]{2,1,0:T(1,128)}), f32[16,1,1024]{2,1,0:T(1,128)S(1)}, u32[]{:S(2)}, u32[]{:S(2)}) async-start(f32[16,1,1024]{2,1,0:T(1,128)} %reshape.118), calls=%async_computation.8 | async-start | bytes 131072 | tf_op jit(solution)/shard_map/all_to_all | solution.py:103
  299.7 5.8 %all-to-all-done.8 = f32[16,1,1024]{2,1,0:T(1,128)S(1)} async-done(((f32[16,1,1024]{2,1,0:T(1,128)}), f32[16,1,1024]{2,1,0:T(1,128)S(1)}, u32[]{:S(2)}, u32[]{:S(2)}) %all-to-all-start.8) | async-done | bytes 65568 | tf_op jit(solution)/shard_map/all_to_all | solution.py:103
  305.5 10.4 %all_to_all.87 = f32[16,1,1024]{2,1,0:T(1,128)S(1)} all-to-all(f32[16,1,1024]{2,1,0:T(1,128)S(1)} %reshape.115), channel_id=1, replica_groups=mesh['near'=2,'x'=4,'z'=8,'far'=2,'core'=2] {'z','core'}, dimensions={0} | all-to-all | bytes 131072 | tf_op jit(solution)/shard_map/all_to_all | solution.py:103
  315.9 3.6 all-to-all-start.4
  319.5 21.5 %all-to-all-done.4 = f32[128,8,384]{2,1,0:T(8,128)S(1)} async-done(((f32[128,8,384]{2,1,0:T(8,128)}), f32[128,8,384]{2,1,0:T(8,128)S(1)}, u32[]{:S(2)}, u32[]{:S(2)}) %all-to-all-start.4) | async-done | bytes 1572896 | tf_op jit(solution)/shard_map/all_to_all | solution.py:103
  342.1 5.6 %all-to-all-start.12 = ((f32[16,16,1024]{2,1,0:T(8,128)}), f32[16,16,1024]{2,1,0:T(8,128)S(1)}, u32[]{:S(2)}, u32[]{:S(2)}) async-start(f32[16,16,1024]{2,1,0:T(8,128)} %broadcast_in_dim.11), calls=%async_computation.12 | async-start | bytes 2097152 | tf_op jit(solution)/shard_map/all_to_all | solution.py:103
  350.1 15.0 %all-to-all-done.12 = f32[16,16,1024]{2,1,0:T(8,128)S(1)} async-done(((f32[16,16,1024]{2,1,0:T(8,128)}), f32[16,16,1024]{2,1,0:T(8,128)S(1)}, u32[]{:S(2)}, u32[]{:S(2)}) %all-to-all-start.12) | async-done | bytes 1048608 | tf_op jit(solution)/shard_map/all_to_all | solution.py:103
  (58 shorter events, 35.2 us)
Async XLA Ops:
  0.6 1.2 copy-start
  1.9 1.4 copy-start.5
  5.1 1.1 copy-start.4
  6.2 13.2 %copy-start.1 = (f32[512,512]{1,0:T(8,128)S(1)}, f32[512,512]{1,0:T(8,128)}, u32[]{:S(2)}) copy-start(f32[512,512]{1,0:T(8,128)} %s_ref.7) | copy-start | bytes 3145732
  6.2 52.9 %all-to-all-start = ((f32[64,2,8,384]{3,2,1,0:T(8,128)}), f32[64,2,8,384]{3,2,1,0:T(8,128)S(1)}, u32[]{:S(2)}, u32[]{:S(2)}) async-start(f32[64,2,8,384]{3,2,1,0:T(8,128)} %copy-done.4), calls=%async_computation | async-start | bytes 3145728 | tf_op jit(solution)/shard_map/all_to_all | solution.py:103
  19.4 1.4 copy-start.7
  20.8 1.4 copy-start.9
  24.0 1.1 copy-start.3
  25.2 40.8 %copy-start.13 = (f32[128,128]{1,0:T(8,128)S(1)}, f32[128,128]{1,0:T(8,128)}, u32[]{:S(2)}) copy-start(f32[128,128]{1,0:T(8,128)} %f_ref.3) | copy-start | bytes 196612
  59.1 45.4 %all-to-all-start.1 = ((f32[64,2,8,384]{3,2,1,0:T(8,128)}), f32[64,2,8,384]{3,2,1,0:T(8,128)}, u32[]{:S(2)}, u32[]{:S(2)}) async-start(f32[64,2,8,384]{3,2,1,0:T(8,128)} %copy-done.3), calls=%async_computation.1 | async-start | bytes 3145728 | tf_op jit(solution)/shard_map/all_to_all | solution.py:103
  74.2 1.1 copy-start.10
  75.4 1.1 copy-start.12
  126.9 1.1 copy-start.11
  184.2 42.1 %all-to-all-start.3 = ((f32[64,2,8,384]{3,2,1,0:T(8,128)}), f32[64,2,8,384]{3,2,1,0:T(8,128)S(1)}, u32[]{:S(2)}, u32[]{:S(2)}) async-start(f32[64,2,8,384]{3,2,1,0:T(8,128)} %bitcast.23), calls=%async_computation.3 | async-start | bytes 3145728 | tf_op jit(solution)/shard_map/all_to_all | solution.py:103
  226.3 16.8 %all-to-all-start.6 = ((f32[16,1,64]{2,1,0:T(1,128)}), f32[16,1,64]{2,1,0:T(1,128)S(1)}, u32[]{:S(2)}, u32[]{:S(2)}) async-start(f32[16,1,64]{2,1,0:T(1,128)} %bitcast.10), calls=%async_computation.6 | async-start | bytes 16384 | tf_op jit(solution)/shard_map/all_to_all | solution.py:103
  229.8 1.4 copy-start.2
  231.2 1.4 copy-start.6
  232.6 3.8 %copy-start.8 = (f32[1,1024,384]{2,1,0:T(8,128)S(1)}, f32[1,1024,384]{2,1,0:T(8,128)}, u32[]{:S(2)}) copy-start(f32[1,1024,384]{2,1,0:T(8,128)} %param.7) | copy-start | bytes 4718596
  243.1 24.7 %all-to-all-start.9 = ((f32[16,16,1024]{2,1,0:T(8,128)}), f32[16,16,1024]{2,1,0:T(8,128)S(1)}, u32[]{:S(2)}, u32[]{:S(2)}) async-start(f32[16,16,1024]{2,1,0:T(8,128)} %all_to_all.66), calls=%async_computation.9 | async-start | bytes 2097152 | tf_op jit(solution)/shard_map/all_to_all | solution.py:103
  268.4 14.3 %all-to-all-start.7 = ((f32[16,1,64]{2,1,0:T(1,128)}), f32[16,1,64]{2,1,0:T(1,128)S(1)}, u32[]{:S(2)}, u32[]{:S(2)}) async-start(f32[16,1,64]{2,1,0:T(1,128)} %reshape.114), calls=%async_computation.7 | async-start | bytes 16384 | tf_op jit(solution)/shard_map/all_to_all | solution.py:103
  282.8 11.3 %all-to-all-start.10 = ((f32[16,1,1024]{2,1,0:T(1,128)}), f32[16,1,1024]{2,1,0:T(1,128)S(1)}, u32[]{:S(2)}, u32[]{:S(2)}) async-start(f32[16,1,1024]{2,1,0:T(1,128)} %all_to_all.68), calls=%async_computation.10 | async-start | bytes 131072 | tf_op jit(solution)/shard_map/all_to_all | solution.py:103
  294.1 11.4 %all-to-all-start.8 = ((f32[16,1,1024]{2,1,0:T(1,128)}), f32[16,1,1024]{2,1,0:T(1,128)S(1)}, u32[]{:S(2)}, u32[]{:S(2)}) async-start(f32[16,1,1024]{2,1,0:T(1,128)} %reshape.118), calls=%async_computation.8 | async-start | bytes 131072 | tf_op jit(solution)/shard_map/all_to_all | solution.py:103
  315.9 25.1 %all-to-all-start.4 = ((f32[128,8,384]{2,1,0:T(8,128)}), f32[128,8,384]{2,1,0:T(8,128)S(1)}, u32[]{:S(2)}, u32[]{:S(2)}) async-start(f32[128,8,384]{2,1,0:T(8,128)} %get-tuple-element.19), calls=%async_computation.4 | async-start | bytes 3145728 | tf_op jit(solution)/shard_map/all_to_all | solution.py:103
  342.1 23.0 %all-to-all-start.12 = ((f32[16,16,1024]{2,1,0:T(8,128)}), f32[16,16,1024]{2,1,0:T(8,128)S(1)}, u32[]{:S(2)}, u32[]{:S(2)}) async-start(f32[16,16,1024]{2,1,0:T(8,128)} %broadcast_in_dim.11), calls=%async_computation.12 | async-start | bytes 2097152 | tf_op jit(solution)/shard_map/all_to_all | solution.py:103
